TPU v7x, 512 devices: a whole 4x8x8 slice. The times are simulated.
512 devices in a mesh: row: 16 (over y, core), col: 32 (over z, x).
Axes of the slice: x: 4, y: 8, z: 8, core: 2. Of those that a mesh axis runs over, the one named last changes fastest.
Arguments:
- feats: bfloat16 [512, 131072], P('col', 'row'), may hold values from -6 to 6
- weight: bfloat16 [512, 512], replicated, may hold values from -0.25 to 0.25
- tile_vals: bfloat16 [16384, 128, 128], P(('row', 'col')), may hold values from -0.125 to 0.125
- tile_src: int32 [512, 32], P(('row', 'col')), may hold values from 0 to 1, as said below
- tile_slot: int32 [512, 32], P(('row', 'col')), may hold values from 0 to 31, as said below
- slot_block: int32 [512, 32], replicated, may hold values from 0 to 63
- cotangent: bfloat16 [512, 131072], P('col', 'row'), may hold values from -6 to 6
Outputs:
- mixed: bfloat16 [512, 131072], P('col', 'row')
- feat_grad: bfloat16 [512, 131072], P('col', 'row')
- weight_grad: float32 [512, 512], replicated
Inputs may be any that keep to these rules, and one draw needn't show every extreme that they name: The tiles of one device name distinct (tile_src, tile_slot) pairs; slots of the device's own row group are all named. tile_slot // 2 is the destination row group of a tile; some tile of every device names slot 31 and some names slot 0. `slot_block`: two slots may target the same block.
All inputs are finite; a program needn't handle non-finite values.
Results may differ from a plain program's by a relative error of at most 0.007.
Values may be sent and summed in bfloat16 or wider, within the bound.
A program may use at most 128 MiB of HBM per device.

v0:
```python
import math

import jax
import jax.numpy as jnp
from jax import lax
from jax.sharding import PartitionSpec as P


def body(feats, weight, tile_vals, tile_src, tile_slot, slot_block, cotangent):
    row_count = lax.axis_size("row")
    col_count = lax.axis_size("col")
    row_index = lax.axis_index("row")
    panel, group_rows = feats.shape
    width = panel * col_count
    slab_rows = group_rows // col_count
    block = tile_vals.shape[1]
    own_blocks = slab_rows // block
    slot_count = slot_block.shape[1]
    capacity = slot_count // row_count
    group_blocks = col_count * own_blocks
    node_total = group_rows * row_count
    node_slab = lax.all_to_all(feats, "col", split_axis=1, concat_axis=0, tiled=True)
    projected = lax.dot_general(
        node_slab, weight, (((0,), (0,)), ((), ())), preferred_element_type=jnp.float32
    ).astype(jnp.bfloat16)
    sources = tile_src[0]
    targets = tile_slot[0]
    slot_matrix = jnp.zeros((slot_count, block, own_blocks, block), jnp.bfloat16)
    slot_matrix = slot_matrix.at[targets, :, sources, :].set(tile_vals)
    slot_matrix = slot_matrix.reshape(slot_count * block, slab_rows)
    partial_value = lax.dot_general(
        projected, slot_matrix, (((0,), (1,)), ((), ())), preferred_element_type=jnp.float32
    )
    outgoing = partial_value.astype(jnp.bfloat16).reshape(width, row_count, capacity * block)
    incoming = lax.all_to_all(
        lax.all_to_all(outgoing, "row", split_axis=1, concat_axis=1, tiled=True),
        "col",
        split_axis=0,
        concat_axis=2,
        tiled=True,
    )
    incoming = incoming.reshape(panel, row_count * col_count * capacity, block)
    chosen = lax.dynamic_slice_in_dim(slot_block, row_index * capacity, capacity, 1).reshape(-1)
    recv_onehot = (chosen[:, None] == jnp.arange(group_blocks, dtype=jnp.int32)[None, :]).astype(
        jnp.bfloat16
    )
    pre = jnp.einsum(
        "fmi,mb->fbi", incoming, recv_onehot, preferred_element_type=jnp.float32
    ).reshape(panel, group_rows)
    sigma = jax.nn.sigmoid(pre)
    mixed = (pre * sigma).astype(jnp.bfloat16)
    grad_pre = (cotangent.astype(jnp.float32) * sigma * (1.0 + pre * (1.0 - sigma))).astype(
        jnp.bfloat16
    )
    everyone = lax.all_gather(grad_pre, "row", axis=1, tiled=True).reshape(
        panel, row_count * group_blocks, block
    )
    row_slots = lax.dynamic_slice_in_dim(slot_block, row_index * col_count, col_count, 0)
    global_index = (jnp.arange(slot_count, dtype=jnp.int32) // capacity)[
        None, :
    ] * group_blocks + row_slots
    selected = jnp.take(everyone, global_index.reshape(-1), axis=1).reshape(
        panel, col_count, slot_count * block
    )
    returned = lax.all_to_all(selected, "col", split_axis=1, concat_axis=0, tiled=True)
    grad_slots = returned.reshape(width, slot_count * block)
    grad_y = lax.dot_general(
        slot_matrix, grad_slots, (((0,), (1,)), ((), ())), preferred_element_type=jnp.float32
    ).astype(jnp.bfloat16)
    weight_part = jnp.dot(node_slab, grad_y, preferred_element_type=jnp.float32)
    weight_grad = lax.psum(weight_part, ("row", "col")) / math.sqrt(node_total)
    grad_slab = lax.dot_general(
        weight, grad_y, (((1,), (1,)), ((), ())), preferred_element_type=jnp.float32
    ).astype(jnp.bfloat16)
    feat_grad = lax.all_to_all(grad_slab, "col", split_axis=0, concat_axis=1, tiled=True)
    return (mixed, feat_grad, weight_grad)


def solution(mesh):
    placed = (
        P("col", "row"),
        P(),
        P(("row", "col"), None, None),
        P(("row", "col"), None),
        P(("row", "col"), None),
        P(),
        P("col", "row"),
    )
    return jax.shard_map(
        body,
        mesh=mesh,
        in_specs=placed,
        out_specs=(P("col", "row"), P("col", "row"), P()),
        check_vma=False,
    )
```

profile of v0, /device:TPU:1, one launch (start us, length us, event | category | flops | bytes accessed | tf_op | source)
XLA Modules:
  0.0 728.6 jit_solution(12333245607442871599)
XLA Ops:
  7.2 1.7 copy.87
  8.9 13.7 %all-to-all-start = ((bf16[16,32,256]{2,0,1:T(8,128)(2,1)}), bf16[16,32,256]{2,0,1:T(8,128)(2,1)S(1)}, u32[]{:S(2)}, u32[]{:S(2)}) async-start(bf16[16,32,256]{2,0,1:T(8,128)(2,1)} %bitcast.96), calls=%async_computation | async-start | bytes 524288 | tf_op jit(solution)/shard_map/all_to_all | solution.py:22
  23.8 3.9 scatter_fusion
  27.7 3.0 copy.48
  30.8 3.0 all-to-all-done
  33.8 5.2 convolution_convert_fusion
  39.0 2.6 copy.84
  41.6 105.3 %all_to_all.73 = bf16[512,16,256]{2,0,1:T(8,128)(2,1)S(1)} all-to-all(bf16[512,16,256]{2,0,1:T(8,128)(2,1)S(1)} %bitcast.98), channel_id=1, replica_groups=mesh['row'=16,'col'=32] {'row'}, dimensions={1} | all-to-all | bytes 8388608 | tf_op jit(solution)/shard_map/all_to_all | solution.py:36
  146.9 4.4 copy.50
  151.3 5.1 all-to-all-start.2
  156.5 0.7 constant_dynamic-slice_fusion
  157.5 96.5 %all-to-all-done.2 = bf16[512,16,256]{2,1,0:T(8,128)(2,1)} async-done(((bf16[512,16,256]{2,1,0:T(8,128)(2,1)}), bf16[512,16,256]{2,1,0:T(8,128)(2,1)}, u32[]{:S(2)}, u32[]{:S(2)}) %all-to-all-start.2) | async-done | bytes 4194336 | tf_op jit(solution)/shard_map/all_to_all | solution.py:35
  254.0 6.5 copy.85
  260.6 7.1 reshape.148
  267.7 3.1 fusion.17
  270.8 1.2 fusion.15
  272.2 0.8 compare_and_fusion
  273.6 36.7 %all-gather.2.cloned.1.call-done = bf16[16,131072]{1,0:T(8,128)(2,1)} async-done(((bf16[16,8192]{1,0:T(8,128)(2,1)}), bf16[16,131072]{1,0:T(8,128)(2,1)}) %all-gather.2.cloned.1.call-update) | async-done | bytes 4194320 | tf_op jit(solution)/shard_map/all_gather | solution.py:55
  310.3 4.9 copy_bitcast_fusion
  315.2 10.6 %gather_fusion = bf16[1024,16,128]{2,1,0:T(8,128)(2,1)} fusion(bf16[16,1024,128]{2,0,1:T(8,128)(2,1)} %copy_bitcast_fusion, s32[1024]{0:T(1024)S(1)} %broadcast_clamp_fusion), kind=kCustom, calls=%fused_computation | custom fusion | bytes 8392704 | tf_op jit(solution)/shard_map/jit(_take)/gather | solution.py:62
  325.8 5.2 copy.55
  331.0 7.4 %gather.7 = bf16[16,32,4096]{2,1,0:T(8,128)(2,1)} reshape(bf16[16,1024,128]{2,1,0:T(8,128)(2,1)} %copy.55) | data formatting | bytes 8388608 | tf_op jit(solution)/shard_map/jit(_take)/gather | solution.py:62
  338.4 2.7 broadcast_select_fusion
  341.1 2.3 copy.56
  343.4 104.1 %all_to_all.74 = bf16[16,32,4096]{2,0,1:T(8,128)(2,1)S(1)} all-to-all(bf16[16,32,4096]{2,0,1:T(8,128)(2,1)S(1)} %copy.56), channel_id=1, replica_groups=mesh['row'=16,'col'=32] {'col'}, dimensions={1} | all-to-all | bytes 8388608 | tf_op jit(solution)/shard_map/all_to_all | solution.py:65
  447.5 1.4 fusion.5
  449.0 1.3 convolution_bitcast_fusion
  450.8 16.0 %all_to_all.75 = bf16[32,16,256]{2,1,0:T(8,128)(2,1)S(1)} all-to-all(bf16[32,16,256]{2,1,0:T(8,128)(2,1)S(1)} %bitcast.107), channel_id=1, replica_groups=mesh['row'=16,'col'=32] {'col'}, dimensions={0} | all-to-all | bytes 524288 | tf_op jit(solution)/shard_map/all_to_all | solution.py:75
  466.8 0.7 copy.63
  467.5 251.6 %all-reduce.2.cloned.1.call-done = f32[512,512]{0,1:T(8,128)} async-done(((f32[512,512]{0,1:T(8,128)}), f32[512,512]{0,1:T(8,128)}) %all-reduce.2.cloned.1.call-update) | async-done | bytes 1048592 | tf_op jit(solution)/shard_map/psum | solution.py:71
  719.1 1.3 broadcast_multiply_fusion
  720.5 1.3 copy.59
  (24 shorter events, 2.8 us)
Async XLA Ops:
  7.2 26.7 %copy-start = (bf16[512,512]{1,0:T(8,128)(2,1)S(1)}, bf16[512,512]{1,0:T(8,128)(2,1)}, u32[]{:S(2)}) copy-start(bf16[512,512]{1,0:T(8,128)(2,1)} %param.8) | copy-start | bytes 1572868
  8.9 24.9 %all-to-all-start = ((bf16[16,32,256]{2,0,1:T(8,128)(2,1)}), bf16[16,32,256]{2,0,1:T(8,128)(2,1)S(1)}, u32[]{:S(2)}, u32[]{:S(2)}) async-start(bf16[16,32,256]{2,0,1:T(8,128)(2,1)} %bitcast.96), calls=%async_computation | async-start | bytes 524288 | tf_op jit(solution)/shard_map/all_to_all | solution.py:22
  151.3 102.7 %all-to-all-start.2 = ((bf16[512,16,256]{2,1,0:T(8,128)(2,1)}), bf16[512,16,256]{2,1,0:T(8,128)(2,1)}, u32[]{:S(2)}, u32[]{:S(2)}) async-start(bf16[512,16,256]{2,1,0:T(8,128)(2,1)} %copy.50), calls=%async_computation.2 | async-start | bytes 8388608 | tf_op jit(solution)/shard_map/all_to_all | solution.py:35
  156.4 153.9 %all-gather.2.cloned.1.call-start = ((), (), s32[]{:S(2)}) async-start(), calls=%async_computation.5 | async-start | bytes 4456448 | tf_op jit(solution)/shard_map/all_gather | solution.py:55
  267.7 3.1 copy-start.2
  272.0 447.2 %all-reduce.2.cloned.1.call-start = ((), (), s32[]{:S(2)}) async-start(), calls=%async_computation.6 | async-start | bytes 2097152 | tf_op jit(solution)/shard_map/psum | solution.py:71
  343.4 104.1 %copy-start.1 = (bf16[32,128,2,128]{1,0,3,2:T(8,128)(2,1)S(1)}, bf16[32,128,2,128]{1,0,3,2:T(8,128)(2,1)}, u32[]{:S(2)}) copy-start(bf16[32,128,2,128]{1,0,3,2:T(8,128)(2,1)} %copy.48) | copy-start | bytes 6291460
Sparse Core Ops, SparseCore 0:
  272.1 38.1 all-gather.1
  450.4 268.6 all-reduce.1
where the time goes:
time: 730 us; the launch traced here: 729 us
  waiting for transfers between devices  388 us (53%)
  blocking collectives  225 us (31%)
  local copies, waits for them, and re-layouts  63.9 us (9%)
  starting transfers between devices  19.1 us (3%)
  between operations  14.2 us (2%)
  matrix products  11.3 us (2%)
    psum x1, waiting for transfers between devices, body(): weight_grad = lax.psum(weight_part, ('row', 'col')) / math.sqrt(node_total)  252 us
    all_to_all x1, blocking collectives, body(): lax.all_to_all(outgoing, 'row', split_axis=1, concat_axis=1, tiled=True)  105 us
    all_to_all x1, blocking collectives, body(): lax.all_to_all(selected, 'col', split_axis=1, concat_axis=0, tiled=True)  104 us
    all_to_all x1, waiting for transfers between devices, body(): lax.all_to_all(lax.all_to_all(outgoing, 'row', split_axis=1, concat_axis=...  96.5 us
    all_gather x1, waiting for transfers between devices, body(): lax.all_gather(grad_pre, 'row', axis=1, tiled=True)  36.7 us
    gather x3, local copies, waits for them, and re-layouts, body(): jnp.take(everyone, global_index.reshape(-1), axis=1)  23.2 us
    all_to_all x1, blocking collectives, body(): lax.all_to_all(grad_slab, 'col', split_axis=0, concat_axis=1, tiled=True)  16 us
  transfers between devices with their start and end apart: 4, of which 4 were waited for; matrix products, arithmetic and copies ran while one was open for 2% of the time, Pallas kernels for 0%

commit v1 on v0

v1 whole, which is shorter than its diff:
```python
import functools
import math
import types

import jax
import jax.numpy as jnp
from jax import lax
from jax.experimental import pallas as pl
from jax.experimental.pallas import tpu as pltpu
from jax.sharding import PartitionSpec as P

BF = jnp.bfloat16
F32 = jnp.float32
MESH = pl.DeviceIdType.MESH
NK = 2
CAP = 2
BLK = 128
LIMIT = 56 * 1024 * 1024


class Dims:
    def __init__(self, n_row, n_col):
        self.nrow, self.ncol = n_row, n_col
        self.nx = 4 if n_col > 4 else 2
        self.ny, self.nz = n_row // NK, n_col // self.nx
        self.width = 16 * n_col
        self.blocks = 2 * n_col
        self.slots = CAP * n_row
        self.na = NK * n_col
        self.nb = n_row * self.nx
        self.ncol_b = self.nb // NK
        self.slot_devices = n_row * n_col
        assert self.na == self.nb

    def here(self):
        r, c = lax.axis_index("row"), lax.axis_index("col")
        return r, c, r // NK, lax.rem(r, NK), c // self.nx, lax.rem(c, self.nx)


def remote(src, dst, send_sem, recv_sem, row, col):
    return pltpu.make_async_remote_copy(
        src_ref=src,
        dst_ref=dst,
        send_sem=send_sem,
        recv_sem=recv_sem,
        device_id=(row, col),
        device_id_type=MESH,
    )


def drain(ref, sem):
    pltpu.make_async_copy(ref, ref, sem).wait()


def each(start, stop, step):
    def run(i, carry):
        step(i)
        return carry

    lax.fori_loop(start, stop, run, 0)


def greet(barrier, row, col):
    pl.semaphore_signal(barrier, inc=1, device_id=(row, col), device_id_type=MESH)


def tile_of(inv, tiles, group, cap, source):
    at = inv[(group * CAP + cap) * 2 + source]
    value = tiles[jnp.maximum(at, 0)]
    return jnp.where(at >= 0, value, jnp.zeros_like(value))


def ways(n, way, piece):
    return n // 2 if way == piece else (n - 1) // 2


def offset_of(pos, n):
    if pos == 0:
        return n // 2
    return n // 2 - (pos + 1) // 2 if pos % 2 else -(n // 2 - pos // 2)


def pos_of(offset, n):
    if isinstance(offset, int):
        return [p for p in range(n) if (offset_of(p, n) - offset) % n == 0][0]
    return jnp.where(offset > n // 2, 2 * offset - n, jnp.maximum(n - 1 - 2 * offset, 0))


def far_count(n):
    return max(1, n - 3)


def near_start(n):
    return max(1, n - 5)


class Ring:
    def __init__(self, n, me, rows, device, send, recv, recv_gather):
        self.n, self.me, self.half, self.device = n, me, rows // 2, device
        self.send, self.recv, self.recv_gather = send, recv, recv_gather
        self.hops = max(1, n // 2)

    def at(self, way, piece, step):
        return (way * 2 + piece) * self.hops + step

    def rows(self, piece):
        return pl.ds(piece * self.half, self.half)

    def near(self, offset):
        return lax.rem(self.me + offset + self.n, self.n)

    def copies(self):
        return sum(ways(self.n, w, p) for w in range(2) for p in range(2))

    def start(self, src, dst, way, piece, step, recv):
        row, col = self.device(self.near(1 - 2 * way))
        at = self.at(way, piece, step)
        remote(src, dst, self.send.at[0], recv.at[at], row, col).start()

    def reduce_step(self, step, dense, got, stage, last):
        for piece in range(2):
            for way in range(2):
                hops = ways(self.n, way, piece)
                if step >= hops:
                    continue
                to = pos_of((1 - 2 * way) * (hops - step), self.n)
                if (to >= far_count(self.n)) != last:
                    continue
                if step == 0:
                    src = dense.at[to, self.rows(piece)]
                else:
                    old = self.at(way, piece, step - 1)
                    drain(got.at[old], self.recv.at[old])
                    new = self.at(way, piece, step)
                    total = got[old].astype(F32) + dense[to, self.rows(piece)].astype(F32)
                    stage[new] = total.astype(BF)
                    src = stage.at[new]
                self.start(src, got.at[self.at(way, piece, step)], way, piece, step, self.recv)

    def reduce_end(self, piece, got):
        ends = []
        for way in range(2):
            hops = ways(self.n, way, piece)
            if hops:
                at = self.at(way, piece, hops - 1)
                drain(got.at[at], self.recv.at[at])
                ends.append(at)
        return ends

    def gather_step(self, step, piece, held, widen):
        for way in range(2):
            hops = ways(self.n, way, piece)
            if step > hops or hops == 0:
                continue
            src = self.near(-(1 - 2 * way) * step)
            pos = pos_of(-(1 - 2 * way) * step, self.n)
            part = held.at[src, self.rows(piece)]
            if step:
                drain(part, self.recv_gather.at[self.at(way, piece, step - 1)])
            if step < hops:
                self.start(part, part, way, piece, step, self.recv_gather)
            if step:
                widen(src, pos, piece)


def whole_kernel(d, scale, names, *refs):
    m = types.SimpleNamespace(**dict(zip(names, refs)))
    r, c, y, k, z, x = d.here()
    me_a, me_b = k * d.ncol + c, r * d.nx + x
    half = d.width // 2
    send, recv = m.send, m.recv
    barrier = pltpu.get_barrier_semaphore()

    def turn(i, n):
        j = (i + 1) // 2
        return jnp.where(lax.rem(i, 2) == 1, j, lax.rem(n - j, n))

    def peer_col(i):
        to_z = lax.rem(z + turn(i // d.nx, d.nz), d.nz)
        return to_z * d.nx + lax.rem(x + i, d.nx)

    def peer_a(i):
        return lax.rem(k + i // d.ncol, NK), peer_col(lax.rem(i, d.ncol))

    def peer_b(i):
        j = lax.rem(i, d.ncol_b)
        to_y = lax.rem(y + turn(j // d.nx, d.ny), d.ny)
        return to_y * NK + lax.rem(k + i // d.ncol_b, NK), lax.rem(x + j, d.nx)

    def hello(i):
        to_k, to_col = peer_a(i)
        greet(barrier, y * NK + to_k, to_col)
        to_row, to_x = peer_b(i)
        greet(barrier, to_row, z * d.nx + to_x)

    each(1, d.na, hello)

    def place(group):
        offset = lax.rem(group // NK - y + d.ny, d.ny)
        at = pl.multiple_of((lax.rem(group, NK) * d.ny + pos_of(offset, d.ny)) * BLK, BLK)
        for cap in range(CAP):
            for s in range(2):
                lanes = slice((cap * 2 + s) * BLK, (cap * 2 + s + 1) * BLK)
                m.matrix[pl.ds(at, BLK), lanes] = tile_of(m.inv, m.tiles, group, cap, s)

    pl.semaphore_wait(barrier, d.na - 1 + d.nb - 1)

    def nodes_of(col):
        return m.feats.at[:, pl.ds(pl.multiple_of(col * 256, 256), 256)]

    own_rows = m.slab.at[pl.ds(pl.multiple_of(c * 16, 16), 16)]
    pltpu.make_async_copy(nodes_of(c), own_rows, recv.at[0]).start()

    def send_feats(i):
        to = peer_col(i)
        remote(nodes_of(to), own_rows, send.at[0], recv.at[0], r, to).start()

    each(1, d.ncol, send_feats)
    each(0, d.nrow, place)
    m.weight_t[...] = m.weight[...].T
    drain(m.slab, recv.at[0])
    value = jnp.dot(m.weight_t[...], m.slab[...], preferred_element_type=F32)
    value = value.reshape(d.ncol, 2, 8, 256)
    value = jnp.concatenate([value[:, 0], value[:, 1]], axis=0)
    m.proj[...] = value.reshape(d.width, 256).astype(BF)

    far_a, far_b = far_count(d.ny), far_count(d.nz)
    lanes_of = [
        pl.ds(pl.multiple_of(pos_of(lax.rem(j - z + d.nz, d.nz), d.nz) * BLK, BLK), BLK)
        for j in range(d.nz)
    ]
    x_of = [lax.rem(x + j, d.nx) for j in range(d.nx)]

    def send_b(group, late):
        lanes = pl.ds(far_b * BLK, (d.nz - far_b) * BLK) if late else pl.ds(0, far_b * BLK)
        sem = 3 if late else 2

        def send_to(to_x):
            src = m.out_b.at[group * d.nx + to_x, :, lanes]
            dst = m.got_b.at[pl.ds(pl.multiple_of(me_b * 16, 16), 16), lanes]
            remote(src, dst, send.at[sem], recv.at[sem], group, z * d.nx + to_x).start()

        @pl.when(group != r)
        def _():
            send_to(x)

        for j in range(1, d.nx):
            send_to(x_of[j])

    def group_step(gk, pos):
        gy = lax.rem(y + offset_of(pos, d.ny) + d.ny, d.ny)
        group = gy * NK + gk
        at = pl.multiple_of((gk * d.ny + pos) * BLK, BLK)
        both = jnp.concatenate(
            [m.matrix[pl.ds(at, BLK), : 2 * BLK], m.matrix[pl.ds(at, BLK), 2 * BLK :]], axis=0
        )
        part = lax.dot_general(
            m.proj[...], both, (((1,), (1,)), ((), ())), preferred_element_type=F32
        )
        first = part[:, :BLK].reshape(2 * d.ncol, 8, BLK)
        second = part[:, BLK:].reshape(2 * d.ncol, 8, BLK)
        packed = jnp.concatenate([first, second], axis=1).astype(BF)
        m.out_a[pl.ds(gk * d.ncol, d.ncol), pos] = packed[: d.ncol]
        for to_x in range(d.nx):
            for to_z in range(d.nz):
                m.out_b[group * d.nx + to_x, :, lanes_of[to_z]] = packed[
                    d.ncol + to_z * d.nx + to_x
                ]
        send_b(group, False)

    def send_a(i, late):
        to_k, to = peer_a(i)
        part = pl.ds(far_a, d.ny - far_a) if late else pl.ds(0, far_a)
        sem = 12 if late else 1
        remote(
            m.out_a.at[to_k * d.ncol + to, part],
            m.got_a.at[part, pl.ds(pl.multiple_of(me_a * 16, 16), 16)],
            send.at[sem], recv.at[sem], y * NK + to_k, to,
        ).start()

    for late in range(2):
        for first_k in range(2):
            gk = k if first_k == 0 else 1 - k
            for pos in range(far_a, d.ny) if late else range(far_a):
                group_step(gk, pos)
            if not late:
                each(max(1, first_k * d.ncol), (first_k + 1) * d.ncol, lambda i: send_a(i, False))
    each(0, d.nrow, lambda i: send_b(lax.rem(r + i, d.nrow), True))
    each(1, d.na, lambda i: send_a(i, True))
    for late in range(2):
        part = pl.ds(far_a, d.ny - far_a) if late else pl.ds(0, far_a)
        pltpu.make_async_copy(
            m.out_a.at[me_a, part],
            m.got_a.at[part, pl.ds(pl.multiple_of(me_a * 16, 16), 16)],
            recv.at[12 if late else 1],
        ).start()
        lanes = pl.ds(far_b * BLK, (d.nz - far_b) * BLK) if late else pl.ds(0, far_b * BLK)
        pltpu.make_async_copy(
            m.out_b.at[me_b, :, lanes],
            m.got_b.at[pl.ds(pl.multiple_of(me_b * 16, 16), 16), lanes],
            recv.at[3 if late else 2],
        ).start()

    lane = lax.broadcasted_iota(jnp.int32, (d.slot_devices, d.na * 16), 1)
    device = lax.broadcasted_iota(jnp.int32, (d.slot_devices, d.na * 16), 0)
    src = lane // 16
    table = m.slot_table[...].astype(F32).astype(BF)
    row_lane = lax.broadcasted_iota(jnp.int32, (1, d.na * 16), 1)
    slot_id = lax.broadcasted_iota(jnp.int32, (d.slots, d.na * 16), 0)
    slot_lane = lax.broadcasted_iota(jnp.int32, (d.slots, d.na * 16), 1)
    lane_cap = lax.rem(slot_lane, 16) // 8
    feature = lax.rem(row_lane, 8).astype(F32)

    def targets(owner):
        onehot = jnp.where(device == owner, 1.0, 0.0).astype(BF)
        m.spread_slots[...] = lax.dot_general(
            table, onehot, (((0,), (0,)), ((), ())), preferred_element_type=F32
        )

    def target_row(group):
        wanted = slot_id == group * CAP + lane_cap
        block = jnp.sum(jnp.where(wanted, m.spread_slots[...], 0.0), axis=0, keepdims=True)
        return block * 8.0 + feature

    targets((src // d.nx) * d.ncol + z * d.nx + lax.rem(src, d.nx))
    m.to_row[d.ny] = target_row(r)
    targets(y * d.na + src)

    for pos in range(d.ny):
        gy = lax.rem(y + offset_of(pos, d.ny) + d.ny, d.ny)
        m.to_row[pos] = target_row(gy * NK + k)
    dense_rows = d.blocks * 8
    row_id = lax.broadcasted_iota(jnp.int32, (dense_rows, d.na * 16), 0).astype(F32)

    def selector(at):
        return jnp.where(row_id == m.to_row[at], 1.0, 0.0).astype(BF)

    m.pick_b[...] = selector(d.ny)

    def keep_pick(pos):
        m.pick_a[pos] = selector(pos)

    each(0, d.ny, keep_pick)
    ring_a = Ring(d.ny, y, dense_rows, lambda j: (j * NK + k, c), m.send_ra, m.recv_ra, m.recv_ga)
    ring_b = Ring(d.nz, z, dense_rows, lambda j: (r, j * d.nx + x), m.send_rb, m.recv_rb, m.recv_gb)

    def aggregate_a(pos):
        m.dense_a[pos] = jnp.dot(
            m.pick_a[pos], m.got_a[pos], preferred_element_type=F32
        ).astype(BF)

    def aggregate_b(first, stop):
        lanes = slice(first * BLK, stop * BLK)
        total = jnp.dot(m.pick_b[...], m.got_b[:, lanes], preferred_element_type=F32).astype(BF)
        for pos in range(first, stop):
            m.dense_b[pos] = total[:, (pos - first) * BLK : (pos - first + 1) * BLK]

    def rings(last):
        for step in range(max(d.ny, d.nz) // 2):
            ring_b.reduce_step(step, m.dense_b, m.ring_got_b, m.stage_b, last)
            ring_a.reduce_step(step, m.dense_a, m.ring_got_a, m.stage_a, last)

    drain(m.got_b.at[:, pl.ds(0, far_b * BLK)], recv.at[2])
    aggregate_b(0, far_b)
    drain(m.got_a.at[pl.ds(0, far_a)], recv.at[1])
    each(0, far_a, aggregate_a)
    rings(False)
    drain(m.got_b.at[:, pl.ds(far_b * BLK, (d.nz - far_b) * BLK)], recv.at[3])
    aggregate_b(far_b, d.nz)
    drain(m.got_a.at[pl.ds(far_a, d.ny - far_a)], recv.at[12])
    each(far_a, d.ny, aggregate_a)
    rings(True)

    def widen_a(src, pos, piece):
        n = d.blocks // 2
        m.wide_a[pl.ds(pos * d.blocks + piece * n, n)] = (
            m.all_a[src, ring_a.rows(piece)].astype(F32).reshape(n, 8, BLK)
        )

    def widen_b(src, pos, piece):
        n = d.blocks // 2
        m.wide_b[pl.ds(pos * d.blocks + piece * n, n)] = (
            m.all_b[src, ring_b.rows(piece)].astype(F32).reshape(n, 8, BLK)
        )

    for piece in range(2):
        ends_b = ring_b.reduce_end(piece, m.ring_got_b)
        ends_a = ring_a.reduce_end(piece, m.ring_got_a)
        first = piece * d.blocks // 4

        def activate(p):
            rows = pl.ds(pl.multiple_of(p * 16, 16), 16)
            local = pl.ds(pl.multiple_of((p - first) * 16, 16), 16)
            sum_a = m.dense_a[d.ny - 1, rows].astype(F32)
            for at in ends_a:
                sum_a += m.ring_got_a[at, local].astype(F32)
            sum_b = m.dense_b[d.nz - 1, rows].astype(F32)
            for at in ends_b:
                sum_b += m.ring_got_b[at, local].astype(F32)
            low, high = [], []
            for part in range(2):
                pick = slice(part * 8, part * 8 + 8)
                pre = jnp.concatenate([sum_a[pick], sum_b[pick]], axis=0)
                lanes = pl.ds(pl.multiple_of((p * 2 + part) * BLK, BLK), BLK)
                sigma = jax.nn.sigmoid(pre)
                m.mixed[:, lanes] = (pre * sigma).astype(BF)
                grad = m.cotangent[:, lanes].astype(F32) * sigma * (1.0 + pre * (1.0 - sigma))
                low.append(grad[:8])
                high.append(grad[8:])
            m.all_a[y, rows] = jnp.concatenate(low, axis=0).astype(BF)
            m.all_b[z, rows] = jnp.concatenate(high, axis=0).astype(BF)

        each(first, first + d.blocks // 4, activate)
        ring_a.gather_step(0, piece, m.all_a, widen_a)
        ring_b.gather_step(0, piece, m.all_b, widen_b)
        widen_a(y, d.ny - 1, piece)
        widen_b(z, d.nz - 1, piece)

    def gathers(step):
        for piece in range(2):
            ring_a.gather_step(step, piece, m.all_a, widen_a)
            ring_b.gather_step(step, piece, m.all_b, widen_b)

    near_a, near_b = near_start(d.ny), near_start(d.nz)

    def columns(far):
        if far:
            return pl.ds(pl.multiple_of(k * d.ny * BLK, BLK), near_a * BLK)
        at = pl.multiple_of((k * d.ny + near_a) * BLK, BLK)
        return pl.ds(at, (d.ny - near_a) * BLK)

    def column(to_y):
        pos = pos_of(lax.rem(y - to_y + d.ny, d.ny), d.ny)
        return pl.ds(pl.multiple_of((k * d.ny + pos) * BLK, BLK), BLK)

    def message(i, far):
        to_k, to_col = peer_a(i)
        to_row, to_x = peer_b(i)
        a, b = to_k * d.ncol + to_col, to_row * d.nx + to_x
        first, stop = (0, near_a) if far else (near_a, d.ny)
        base = ((y * NK + to_k) * d.ncol + to_col) * d.slots + k * CAP
        for pos in range(first, stop):
            slot = base + group_slot[pos]
            rows = [
                m.wide_a[pos * d.blocks + m.slot_flat[slot + cap]] for cap in range(CAP)
            ]
            m.back_a[a, :, pos * BLK : (pos + 1) * BLK] = jnp.concatenate(rows, axis=0).astype(BF)
        src_a = m.back_a.at[a, :, pl.ds(first * BLK, (stop - first) * BLK)]
        dst_a = m.grads_a.at[pl.ds(pl.multiple_of(c * 16, 16), 16), columns(far)]
        first, stop = (0, near_b) if far else (near_b, d.nz)
        base = (to_row * d.ncol + z * d.nx + to_x) * d.slots
        at = [m.slot_flat[base + r * CAP + cap] for cap in range(CAP)]
        for pos in range(first, stop):
            rows = [m.wide_b[pos * d.blocks + at[cap]] for cap in range(CAP)]
            m.back_b[b, pos * 16 : pos * 16 + 16] = jnp.concatenate(rows, axis=0).astype(BF)
        src_b = m.back_b.at[b, pl.ds(first * 16, (stop - first) * 16)]
        to_rows = pl.ds(pl.multiple_of((x * d.nz + first) * 16, 16), (stop - first) * 16)
        dst_b = m.grads_b.at[to_rows, column(to_row // NK)]
        return src_a, dst_a, y * NK + to_k, to_col, src_b, dst_b, to_row, z * d.nx + to_x

    group_slot = [
        lax.rem(y + offset_of(pos, d.ny) + d.ny, d.ny) * NK * CAP for pos in range(d.ny)
    ]

    def give(far):
        sem_a, sem_b = (13, 14) if far else (4, 5)

        def run(i):
            src_a, dst_a, row_a, col_a, src_b, dst_b, row_b, col_b = message(i, far)
            remote(src_a, dst_a, send.at[sem_a], recv.at[sem_a], row_a, col_a).start()
            remote(src_b, dst_b, send.at[sem_b], recv.at[sem_b], row_b, col_b).start()

        return run

    def keep(far):
        sem_a, sem_b = (13, 14) if far else (4, 5)
        src_a, dst_a, _, _, src_b, dst_b, _, _ = message(0, far)
        pltpu.make_async_copy(src_a, dst_a, recv.at[sem_a]).start()
        pltpu.make_async_copy(src_b, dst_b, recv.at[sem_b]).start()

    top = max(d.ny, d.nz) // 2
    for step in range(1, min(2, top) + 1):
        gathers(step)
    each(1, d.na // 4, give(False))
    if top >= 3:
        gathers(3)
    each(d.na // 4, d.na // 2, give(False))
    if top >= 4:
        gathers(4)
    each(d.na // 2, d.na, give(False))
    each(1, d.na, give(True))
    keep(False)
    keep(True)

    span = d.ny * BLK
    drain(m.grads_a.at[:, pl.ds(0, NK * (d.ny - near_a) * BLK)], recv.at[4])
    for half_k in range(NK):
        lanes = slice(half_k * span + near_a * BLK, (half_k + 1) * span)
        value = jnp.dot(m.grads_a[:, lanes], m.matrix[lanes, :], preferred_element_type=F32)
        m.wide[0] = value if half_k == 0 else m.wide[0] + value
    drain(m.grads_b.at[pl.ds(0, d.nx * (d.nz - near_b) * 16)], recv.at[5])
    for to_x in range(d.nx):
        rows = slice((to_x * d.nz + near_b) * 16, (to_x + 1) * d.nz * 16)
        m.wide[1, rows] = jnp.dot(m.grads_b[rows], m.matrix[...], preferred_element_type=F32)
    drain(m.grads_a.at[:, pl.ds(0, NK * near_a * BLK)], recv.at[13])
    for half_k in range(NK):
        lanes = slice(half_k * span, half_k * span + near_a * BLK)
        m.wide[0] += jnp.dot(m.grads_a[:, lanes], m.matrix[lanes, :], preferred_element_type=F32)
    drain(m.grads_b.at[pl.ds(0, d.nx * near_b * 16)], recv.at[14])
    for to_x in range(d.nx):
        rows = slice(to_x * d.nz * 16, (to_x * d.nz + near_b) * 16)
        m.wide[1, rows] = jnp.dot(m.grads_b[rows], m.matrix[...], preferred_element_type=F32)

    def join(path):
        value = m.wide[path].reshape(d.ncol, CAP, 8, 4 * BLK)
        return value[:, 0, :, : 2 * BLK] + value[:, 1, :, 2 * BLK :]

    m.joined[:, 0] = join(0)
    high = join(1).reshape(d.nx, d.nz, 8, 256)
    for pos in range(d.nz):
        to_z = lax.rem(z + offset_of(pos, d.nz) + d.nz, d.nz)
        m.joined[pl.ds(to_z * d.nx, d.nx), 1] = high[:, pos]
    m.grad_y[...] = m.joined[...].reshape(d.width, 256).astype(BF)

    part = lax.dot_general(
        m.slab[...], m.grad_y[...], (((1,), (1,)), ((), ())), preferred_element_type=F32
    )
    m.parts[0] = part[:, :half]
    m.parts[1] = part[:, half:]
    twin_row = y * NK + (1 - k)
    swap = remote(m.parts.at[1 - k], m.twin, send.at[6], recv.at[6], twin_row, c)
    swap.start()
    m.grad_slab[...] = jnp.dot(
        m.weight[...], m.grad_y[...], preferred_element_type=F32
    ).astype(BF)
    swap.wait()
    m.summed[...] = (m.parts[k] + m.twin[...]).astype(BF)

    def rows_of(ref, col):
        return ref.at[pl.ds(pl.multiple_of(col * 16, 16), 16)]

    own_nodes = m.feat_grad.at[:, pl.ds(pl.multiple_of(c * 256, 256), 256)]
    pltpu.make_async_copy(rows_of(m.summed, c), m.spread.at[c], recv.at[7]).start()
    pltpu.make_async_copy(rows_of(m.grad_slab, c), own_nodes, recv.at[8]).start()

    def scatter(i):
        to = peer_col(i)
        remote(rows_of(m.summed, to), m.spread.at[c], send.at[7], recv.at[7], r, to).start()

    def features(i):
        to = peer_col(i)
        remote(rows_of(m.grad_slab, to), own_nodes, send.at[8], recv.at[8], r, to).start()

    each(1, d.ncol, scatter)
    each(1, d.ncol, features)
    drain(m.spread, recv.at[7])
    total = m.spread[0].astype(F32)
    for j in range(1, d.ncol):
        total += m.spread[j].astype(F32)
    m.mine[...] = total
    pltpu.make_async_copy(m.mine, m.rows_all.at[y], recv.at[9]).start()

    def along_y(i):
        to = lax.rem(y + i, d.ny)
        remote(m.mine, m.rows_all.at[y], send.at[9], recv.at[9], to * NK + k, c).start()

    each(1, d.ny, along_y)
    drain(m.rows_all, recv.at[9])
    total = m.rows_all[0]
    for j in range(1, d.ny):
        total += m.rows_all[j]
    m.final[...] = (total * scale).astype(BF)
    own_rows_w = m.whole.at[k, pl.ds(pl.multiple_of(c * 16, 16), 16)]
    pltpu.make_async_copy(m.final, own_rows_w, recv.at[10]).start()

    def publish(i):
        to = peer_col(i)
        remote(m.final, own_rows_w, send.at[10], recv.at[10], r, to).start()

    each(1, d.ncol, publish)
    drain(m.whole.at[k], recv.at[10])
    share = remote(m.whole.at[k], m.whole.at[k], send.at[11], recv.at[11], twin_row, c)
    share.start()
    share.wait()
    m.weight_grad[:, :half] = m.whole[0].astype(F32)
    m.weight_grad[:, half:] = m.whole[1].astype(F32)
    drain(m.slab.at[pl.ds(0, d.width - 16)], send.at[0])
    rest = pl.ds(0, d.na - 1)
    drain(m.out_a.at[rest, pl.ds(0, far_a)], send.at[1])
    drain(m.out_a.at[rest, pl.ds(far_a, d.ny - far_a)], send.at[12])
    drain(m.out_b.at[rest, :, pl.ds(0, far_b * BLK)], send.at[2])
    drain(m.out_b.at[rest, :, pl.ds(far_b * BLK, (d.nz - far_b) * BLK)], send.at[3])
    for ring, got, sem in ((ring_a, m.ring_got_a, m.send_ra), (ring_b, m.ring_got_b, m.send_rb)):
        for _ in range(2):
            drain(got.at[pl.ds(0, ring.copies())], sem.at[0])
    drain(m.back_a.at[rest, :, pl.ds(near_a * BLK, (d.ny - near_a) * BLK)], send.at[4])
    drain(m.back_a.at[rest, :, pl.ds(0, near_a * BLK)], send.at[13])
    drain(m.back_b.at[rest, pl.ds(near_b * 16, (d.nz - near_b) * 16)], send.at[5])
    drain(m.back_b.at[rest, pl.ds(0, near_b * 16)], send.at[14])
    drain(m.spread.at[pl.ds(0, d.ncol - 1)], send.at[7])
    drain(m.grad_slab.at[pl.ds(0, d.width - 16)], send.at[8])
    drain(m.rows_all.at[pl.ds(0, d.ny - 1)], send.at[9])
    drain(m.whole.at[0, pl.ds(0, d.width - 16)], send.at[10])
    drain(m.grad_slab, recv.at[8])


def body(d, node_total, feats, weight, tile_vals, tile_src, tile_slot, slot_block, cotangent):
    vmem = pl.BlockSpec(memory_space=pltpu.VMEM)
    smem = pl.BlockSpec(memory_space=pltpu.SMEM)
    anywhere = pl.BlockSpec(memory_space=pl.ANY)
    sds = jax.ShapeDtypeStruct
    pair = tile_slot[0] * 2 + tile_src[0]
    pair_ids = jnp.arange(2 * d.slots, dtype=jnp.int32)
    tile_ids = jnp.arange(tile_vals.shape[0], dtype=jnp.int32)
    inv = jnp.max(jnp.where(pair[:, None] == pair_ids[None, :], tile_ids[:, None], -1), axis=0)
    inputs = dict(
        inv=(inv, smem),
        slot_flat=(slot_block.reshape(-1), smem),
        slot_table=(slot_block, vmem),
        feats=(feats, vmem),
        weight=(weight, vmem),
        tiles=(tile_vals, vmem),
        cotangent=(cotangent, vmem),
    )
    outputs = dict(
        mixed=(sds(cotangent.shape, BF), vmem),
        feat_grad=(sds(feats.shape, BF), anywhere),
        weight_grad=(sds((d.width, d.width), F32), vmem),
    )
    half, dense_rows, hops_a, hops_b = d.width // 2, d.blocks * 8, max(1, d.ny // 2), max(1, d.nz // 2)
    dma = pltpu.SemaphoreType.DMA
    scratch = dict(
        slab=((d.width, 256), BF),
        weight_t=((d.width, d.width), BF),
        proj=((d.width, 256), BF),
        matrix=((d.nrow * BLK, 4 * BLK), BF),
        out_a=((d.na, d.ny, 16, BLK), BF),
        out_b=((d.nb, 16, d.nz * BLK), BF),
        got_a=((d.ny, d.na * 16, BLK), BF),
        got_b=((d.nb * 16, d.nz * BLK), BF),
        spread_slots=((d.slots, d.na * 16), F32),
        to_row=((d.ny + 1, 1, d.na * 16), F32),
        joined=((d.ncol, 2, 8, 256), F32),
        pick_a=((d.ny, dense_rows, d.na * 16), BF),
        pick_b=((dense_rows, d.nb * 16), BF),
        dense_a=((d.ny, dense_rows, BLK), BF),
        dense_b=((d.nz, dense_rows, BLK), BF),
        ring_got_a=((4 * hops_a, dense_rows // 2, BLK), BF),
        ring_got_b=((4 * hops_b, dense_rows // 2, BLK), BF),
        stage_a=((4 * hops_a, dense_rows // 2, BLK), BF),
        stage_b=((4 * hops_b, dense_rows // 2, BLK), BF),
        all_a=((d.ny, dense_rows, BLK), BF),
        all_b=((d.nz, dense_rows, BLK), BF),
        wide_a=((d.ny * d.blocks, 8, BLK), F32),
        wide_b=((d.nz * d.blocks, 8, BLK), F32),
        back_a=((d.na, 16, d.ny * BLK), BF),
        back_b=((d.nb, d.nz * 16, BLK), BF),
        grads_a=((d.width, d.nrow * BLK), BF),
        grads_b=((d.width, d.nrow * BLK), BF),
        wide=((2, d.width, 4 * BLK), F32),
        grad_y=((d.width, 256), BF),
        grad_slab=((d.width, 256), BF),
        parts=((2, d.width, half), F32),
        twin=((d.width, half), F32),
        summed=((d.width, half), BF),
        spread=((d.ncol, 16, half), BF),
        mine=((16, half), F32),
        rows_all=((d.ny, 16, half), F32),
        final=((16, half), BF),
        whole=((2, d.width, half), BF),
    )
    semaphores = dict(
        send=15, recv=15, send_ra=1, send_rb=1, recv_ra=4 * hops_a, recv_rb=4 * hops_b
    )
    semaphores.update(recv_ga=4 * hops_a, recv_gb=4 * hops_b)
    names = tuple(inputs) + tuple(outputs) + tuple(scratch) + tuple(semaphores)
    return pl.pallas_call(
        functools.partial(whole_kernel, d, 1.0 / math.sqrt(node_total), names),
        out_shape=tuple(v[0] for v in outputs.values()),
        in_specs=[v[1] for v in inputs.values()],
        out_specs=tuple(v[1] for v in outputs.values()),
        scratch_shapes=[pltpu.VMEM(*v) for v in scratch.values()]
        + [dma((n,)) for n in semaphores.values()],
        compiler_params=pltpu.CompilerParams(
            collective_id=0, has_side_effects=True, vmem_limit_bytes=LIMIT
        ),
        name="layer",
    )(*(v[0] for v in inputs.values()))


def solution(mesh):
    d = Dims(mesh.shape["row"], mesh.shape["col"])
    placed = (
        P("col", "row"),
        P(),
        P(("row", "col"), None, None),
        P(("row", "col"), None),
        P(("row", "col"), None),
        P(),
        P("col", "row"),
    )
    node_total = d.nrow * d.ncol * 2 * BLK
    return jax.shard_map(
        functools.partial(body, d, node_total),
        mesh=mesh,
        in_specs=placed,
        out_specs=(P("col", "row"), P("col", "row"), P()),
        check_vma=False,
    )
```

time: 730 us -> 197 us (0.27)
  waiting for transfers between devices: 388 us -> 0 us
  blocking collectives: 225 us -> 0 us
  Pallas kernels: 0 us -> 189 us
  local copies, waits for them, and re-layouts: 63.9 us -> 6.11 us
  starting transfers between devices: 19.1 us -> 0 us
  between operations: 14.2 us -> 0.67 us
  matrix products: 11.3 us -> 0 us
    psum x1 -> x0, waiting for transfers between devices: 252 us -> none  [body(): weight_grad = lax.psum(weight_part, ('row', 'col')) / math.sqrt(node_total)]
    all_to_all x3 -> x0, blocking collectives: 225 us -> none  [the longest x1 105 us: body(): lax.all_to_all(outgoing, 'row', split_axis=1, concat_axis=1, tiled=True)]
    pallas_call x0 -> x1, Pallas kernels: none -> 189 us  [body(): pl.pallas_call(functools.partial(whole_kernel, d, 1.0 / math.sqrt(node_to...]
    all_to_all x2 -> x0, waiting for transfers between devices: 99.6 us -> none  [the longest x1 96.5 us: body(): lax.all_to_all(lax.all_to_all(outgoing, 'row', split_axis=1, concat_axis=...]
    all_gather x1 -> x0, waiting for transfers between devices: 36.7 us -> none  [body(): lax.all_gather(grad_pre, 'row', axis=1, tiled=True)]
    gather x3 -> x0, local copies, waits for them, and re-layouts: 23.2 us -> none  [body(): jnp.take(everyone, global_index.reshape(-1), axis=1)]
    all_to_all x2 -> x0, starting transfers between devices: 18.8 us -> none  [the longest x1 13.7 us: body(): lax.all_to_all(feats, 'col', split_axis=1, concat_axis=0, tiled=True)]
    reshape x4 -> x1, local copies, waits for them, and re-layouts: 14.6 us -> 0.75 us  [body(): slot_block.reshape(-1)]
  transfers between devices with their start and end apart: 4 -> 0, of which waited for: 4 -> 0; matrix products, arithmetic and copies ran while one was open for 2% -> 0% of each run, Pallas kernels for 0% -> 0%
where the time goes in v1:
time: 197 us
  Pallas kernels  189 us (96%)
  local copies, waits for them, and re-layouts  6.11 us (3%)
    pallas_call x1, Pallas kernels, body(): pl.pallas_call(functools.partial(whole_kernel, d, 1.0 / math.sqrt(node_to...  189 us
    unnamed x8, local copies, waits for them, and re-layouts  5.37 us

profile of v1, /device:TPU:1, one launch (start us, length us, event | category | flops | bytes accessed | tf_op | source)
XLA Modules:
  0.0 197.2 jit_solution(2626755162673875424)
XLA Ops:
  0.6 0.7 add_bitcast_fusion
  1.3 0.6 select_reduce_fusion.refs_0_
  1.9 1.0 copy.13.refs_2_
  2.9 0.0 copy-start
  2.9 0.7 reshape.22.refs_1_
  3.6 0.0 copy-done
  3.6 189.2 %layer.1 = (bf16[16,8192]{1,0:T(8,128)(2,1)}, bf16[16,8192]{1,0:T(8,128)(2,1)}, f32[512,512]{1,0:T(8,128)}) custom-call(s32[64]{0:T(128)} %select_reduce_fusion.refs_0_, s32[16384]{0:T(1024)} %reshape.22.refs_1_, s32[512,32]{1,0:T(8,128)} %copy-done, bf16[16,8192]{1,0:T(8,128)(2,1)} %refs_3_.1, bf16[512,512]{1,0:T(8,128)(2,1)} %refs_4_.1, ...), custom_call_target="tpu_custom_call" | custom-call | tf_op jit(solution)/shard_map/layer/pallas_call | solution.py:677
  192.8 0.0 copy-start.1
  192.8 1.8 copy.18
  194.6 1.7 copy.19
  196.2 0.0 copy-done.1
  196.2 1.0 copy.20
Async XLA Ops:
  2.9 0.8 copy-start
  192.8 3.4 %copy-start.1 = (f32[512,512]{1,0:T(8,128)S(1)}, f32[512,512]{1,0:T(8,128)}, u32[]{:S(2)}) copy-start(f32[512,512]{1,0:T(8,128)} %get-tuple-element.8) | copy-start | bytes 3145732

commit v2 on v1

--- a/solution.py
+++ b/solution.py
@@ -91,7 +91,7 @@
 
 
 def near_start(n):
-    return max(1, n - 5)
+    return max(1, n - 3)
 
 
 class Ring:
@@ -175,25 +175,45 @@
         j = (i + 1) // 2
         return jnp.where(lax.rem(i, 2) == 1, j, lax.rem(n - j, n))
 
-    def peer_col(i):
-        to_z = lax.rem(z + turn(i // d.nx, d.nz), d.nz)
-        return to_z * d.nx + lax.rem(x + i, d.nx)
-
-    def peer_a(i):
-        return lax.rem(k + i // d.ncol, NK), peer_col(lax.rem(i, d.ncol))
-
-    def peer_b(i):
-        j = lax.rem(i, d.ncol_b)
-        to_y = lax.rem(y + turn(j // d.nx, d.ny), d.ny)
-        return to_y * NK + lax.rem(k + i // d.ncol_b, NK), lax.rem(x + j, d.nx)
-
-    def hello(i):
-        to_k, to_col = peer_a(i)
-        greet(barrier, y * NK + to_k, to_col)
-        to_row, to_x = peer_b(i)
-        greet(barrier, to_row, z * d.nx + to_x)
-
-    each(1, d.na, hello)
+    x_of = [lax.rem(x + j, d.nx) for j in range(d.nx)]
+    k_of = [k, 1 - k]
+
+    def line_a(other, jz, visit):
+        first = isinstance(jz, int)
+        to_z = z if first else lax.rem(z + turn(jz, d.nz), d.nz)
+        for j in range(1 if first and not other else 0, d.nx):
+            visit(y * NK + k_of[other], to_z * d.nx + x_of[j], k_of[other])
+
+    def line_b(other, jy, visit):
+        first = isinstance(jy, int)
+        to_y = y if first else lax.rem(y + turn(jy, d.ny), d.ny)
+        for j in range(1 if first and not other else 0, d.nx):
+            visit(to_y * NK + k_of[other], z * d.nx + x_of[j], to_y, x_of[j])
+
+    def peers_a(other, visit):
+        line_a(other, 0, visit)
+        each(1, d.nz, lambda jz: line_a(other, jz, visit))
+
+    def peers_b(other, visit):
+        line_b(other, 0, visit)
+        each(1, d.ny, lambda jy: line_b(other, jy, visit))
+
+    loads = [
+        pltpu.make_async_copy(src, dst, m.load.at[at])
+        for at, (src, dst) in enumerate(
+            (
+                (m.tiles_in, m.tiles),
+                (m.weight_in, m.weight),
+                (m.slot_table_in, m.slot_table),
+                (m.cotangent_in, m.cotangent),
+            )
+        )
+    ]
+    for load in loads:
+        load.start()
+    for other in range(NK):
+        peers_a(other, lambda row, col, _: greet(barrier, row, col))
+        peers_b(other, lambda row, col, *_: greet(barrier, row, col))
 
     def place(group):
         offset = lax.rem(group // NK - y + d.ny, d.ny)
@@ -211,12 +231,13 @@
     own_rows = m.slab.at[pl.ds(pl.multiple_of(c * 16, 16), 16)]
     pltpu.make_async_copy(nodes_of(c), own_rows, recv.at[0]).start()
 
-    def send_feats(i):
-        to = peer_col(i)
-        remote(nodes_of(to), own_rows, send.at[0], recv.at[0], r, to).start()
-
-    each(1, d.ncol, send_feats)
+    def send_feats(row, col, _):
+        remote(nodes_of(col), own_rows, send.at[0], recv.at[0], row, col).start()
+
+    peers_a(0, send_feats)
+    loads[0].wait()
     each(0, d.nrow, place)
+    loads[1].wait()
     m.weight_t[...] = m.weight[...].T
     drain(m.slab, recv.at[0])
     value = jnp.dot(m.weight_t[...], m.slab[...], preferred_element_type=F32)
@@ -229,7 +250,6 @@
         pl.ds(pl.multiple_of(pos_of(lax.rem(j - z + d.nz, d.nz), d.nz) * BLK, BLK), BLK)
         for j in range(d.nz)
     ]
-    x_of = [lax.rem(x + j, d.nx) for j in range(d.nx)]
 
     def send_b(group, late):
         lanes = pl.ds(far_b * BLK, (d.nz - far_b) * BLK) if late else pl.ds(0, far_b * BLK)
@@ -268,15 +288,16 @@
                 ]
         send_b(group, False)
 
-    def send_a(i, late):
-        to_k, to = peer_a(i)
+    def send_a(late):
         part = pl.ds(far_a, d.ny - far_a) if late else pl.ds(0, far_a)
         sem = 12 if late else 1
-        remote(
-            m.out_a.at[to_k * d.ncol + to, part],
-            m.got_a.at[part, pl.ds(pl.multiple_of(me_a * 16, 16), 16)],
-            send.at[sem], recv.at[sem], y * NK + to_k, to,
-        ).start()
+        dst = m.got_a.at[part, pl.ds(pl.multiple_of(me_a * 16, 16), 16)]
+
+        def visit(row, col, to_k):
+            src = m.out_a.at[to_k * d.ncol + col, part]
+            remote(src, dst, send.at[sem], recv.at[sem], row, col).start()
+
+        return visit
 
     for late in range(2):
         for first_k in range(2):
@@ -284,9 +305,10 @@
             for pos in range(far_a, d.ny) if late else range(far_a):
                 group_step(gk, pos)
             if not late:
-                each(max(1, first_k * d.ncol), (first_k + 1) * d.ncol, lambda i: send_a(i, False))
+                peers_a(first_k, send_a(False))
     each(0, d.nrow, lambda i: send_b(lax.rem(r + i, d.nrow), True))
-    each(1, d.na, lambda i: send_a(i, True))
+    for other in range(NK):
+        peers_a(other, send_a(True))
     for late in range(2):
         part = pl.ds(far_a, d.ny - far_a) if late else pl.ds(0, far_a)
         pltpu.make_async_copy(
@@ -304,6 +326,7 @@
     lane = lax.broadcasted_iota(jnp.int32, (d.slot_devices, d.na * 16), 1)
     device = lax.broadcasted_iota(jnp.int32, (d.slot_devices, d.na * 16), 0)
     src = lane // 16
+    loads[2].wait()
     table = m.slot_table[...].astype(F32).astype(BF)
     row_lane = lax.broadcasted_iota(jnp.int32, (1, d.na * 16), 1)
     slot_id = lax.broadcasted_iota(jnp.int32, (d.slots, d.na * 16), 0)
@@ -314,7 +337,7 @@
     def targets(owner):
         onehot = jnp.where(device == owner, 1.0, 0.0).astype(BF)
         m.spread_slots[...] = lax.dot_general(
-            table, onehot, (((0,), (0,)), ((), ())), preferred_element_type=F32
+            table, onehot, (((1,), (0,)), ((), ())), preferred_element_type=F32
         )
 
     def target_row(group):
@@ -370,6 +393,7 @@
     drain(m.got_a.at[pl.ds(far_a, d.ny - far_a)], recv.at[12])
     each(far_a, d.ny, aggregate_a)
     rings(True)
+    loads[3].wait()
 
     def widen_a(src, pos, piece):
         n = d.blocks // 2
@@ -433,62 +457,73 @@
         pos = pos_of(lax.rem(y - to_y + d.ny, d.ny), d.ny)
         return pl.ds(pl.multiple_of((k * d.ny + pos) * BLK, BLK), BLK)
 
-    def message(i, far):
-        to_k, to_col = peer_a(i)
-        to_row, to_x = peer_b(i)
-        a, b = to_k * d.ncol + to_col, to_row * d.nx + to_x
+    group_slot = [
+        (lax.rem(y + offset_of(pos, d.ny) + d.ny, d.ny) * NK + k) * CAP for pos in range(d.ny)
+    ]
+
+    def give_a(far, row, col, to_k):
         first, stop = (0, near_a) if far else (near_a, d.ny)
-        base = ((y * NK + to_k) * d.ncol + to_col) * d.slots + k * CAP
+        a, device = to_k * d.ncol + col, row * d.ncol + col
         for pos in range(first, stop):
-            slot = base + group_slot[pos]
             rows = [
-                m.wide_a[pos * d.blocks + m.slot_flat[slot + cap]] for cap in range(CAP)
+                m.wide_a[pos * d.blocks + m.slots[group_slot[pos] + cap, device]]
+                for cap in range(CAP)
             ]
             m.back_a[a, :, pos * BLK : (pos + 1) * BLK] = jnp.concatenate(rows, axis=0).astype(BF)
-        src_a = m.back_a.at[a, :, pl.ds(first * BLK, (stop - first) * BLK)]
-        dst_a = m.grads_a.at[pl.ds(pl.multiple_of(c * 16, 16), 16), columns(far)]
+        src = m.back_a.at[a, :, pl.ds(first * BLK, (stop - first) * BLK)]
+        return src, m.grads_a.at[pl.ds(pl.multiple_of(c * 16, 16), 16), columns(far)]
+
+    def give_b(far, row, col, to_y, to_x):
         first, stop = (0, near_b) if far else (near_b, d.nz)
-        base = (to_row * d.ncol + z * d.nx + to_x) * d.slots
-        at = [m.slot_flat[base + r * CAP + cap] for cap in range(CAP)]
+        b, device = row * d.nx + to_x, row * d.ncol + col
+        at = [m.slots[r * CAP + cap, device] for cap in range(CAP)]
         for pos in range(first, stop):
             rows = [m.wide_b[pos * d.blocks + at[cap]] for cap in range(CAP)]
             m.back_b[b, pos * 16 : pos * 16 + 16] = jnp.concatenate(rows, axis=0).astype(BF)
-        src_b = m.back_b.at[b, pl.ds(first * 16, (stop - first) * 16)]
+        src = m.back_b.at[b, pl.ds(first * 16, (stop - first) * 16)]
         to_rows = pl.ds(pl.multiple_of((x * d.nz + first) * 16, 16), (stop - first) * 16)
-        dst_b = m.grads_b.at[to_rows, column(to_row // NK)]
-        return src_a, dst_a, y * NK + to_k, to_col, src_b, dst_b, to_row, z * d.nx + to_x
-
-    group_slot = [
-        lax.rem(y + offset_of(pos, d.ny) + d.ny, d.ny) * NK * CAP for pos in range(d.ny)
-    ]
-
-    def give(far):
+        return src, m.grads_b.at[to_rows, column(to_y)]
+
+    def give(far, other, start, stop):
         sem_a, sem_b = (13, 14) if far else (4, 5)
 
-        def run(i):
-            src_a, dst_a, row_a, col_a, src_b, dst_b, row_b, col_b = message(i, far)
-            remote(src_a, dst_a, send.at[sem_a], recv.at[sem_a], row_a, col_a).start()
-            remote(src_b, dst_b, send.at[sem_b], recv.at[sem_b], row_b, col_b).start()
-
-        return run
+        def visit_a(row, col, to_k):
+            src, dst = give_a(far, row, col, to_k)
+            remote(src, dst, send.at[sem_a], recv.at[sem_a], row, col).start()
+
+        def visit_b(row, col, to_y, to_x):
+            src, dst = give_b(far, row, col, to_y, to_x)
+            remote(src, dst, send.at[sem_b], recv.at[sem_b], row, col).start()
+
+        def both_lines(j):
+            line_a(other, j, visit_a)
+            line_b(other, j, visit_b)
+
+        if start == 0:
+            both_lines(0)
+        each(max(1, start), stop, both_lines)
 
     def keep(far):
         sem_a, sem_b = (13, 14) if far else (4, 5)
-        src_a, dst_a, _, _, src_b, dst_b, _, _ = message(0, far)
-        pltpu.make_async_copy(src_a, dst_a, recv.at[sem_a]).start()
-        pltpu.make_async_copy(src_b, dst_b, recv.at[sem_b]).start()
-
-    top = max(d.ny, d.nz) // 2
-    for step in range(1, min(2, top) + 1):
-        gathers(step)
-    each(1, d.na // 4, give(False))
+        src, dst = give_a(far, r, c, k)
+        pltpu.make_async_copy(src, dst, recv.at[sem_a]).start()
+        src, dst = give_b(far, r, c, y, x)
+        pltpu.make_async_copy(src, dst, recv.at[sem_b]).start()
+
+    top, mid = max(d.ny, d.nz) // 2, d.ny // 2
+    gathers(1)
+    give(False, 0, 0, mid)
+    if top >= 2:
+        gathers(2)
+    give(False, 0, mid, d.ny)
     if top >= 3:
         gathers(3)
-    each(d.na // 4, d.na // 2, give(False))
+    give(False, 1, 0, mid)
     if top >= 4:
         gathers(4)
-    each(d.na // 2, d.na, give(False))
-    each(1, d.na, give(True))
+    give(False, 1, mid, d.ny)
+    give(True, 0, 0, d.ny)
+    give(True, 1, 0, d.ny)
     keep(False)
     keep(True)
 
@@ -527,63 +562,62 @@
     )
     m.parts[0] = part[:, :half]
     m.parts[1] = part[:, half:]
+    m.to_twin[...] = m.parts[1 - k].astype(BF)
     twin_row = y * NK + (1 - k)
-    swap = remote(m.parts.at[1 - k], m.twin, send.at[6], recv.at[6], twin_row, c)
+    swap = remote(m.to_twin, m.twin, send.at[6], recv.at[6], twin_row, c)
     swap.start()
     m.grad_slab[...] = jnp.dot(
         m.weight[...], m.grad_y[...], preferred_element_type=F32
     ).astype(BF)
     swap.wait()
-    m.summed[...] = (m.parts[k] + m.twin[...]).astype(BF)
-
-    def rows_of(ref, col):
-        return ref.at[pl.ds(pl.multiple_of(col * 16, 16), 16)]
-
+    m.summed[...] = (m.parts[k] + m.twin[...].astype(F32)).astype(BF)
+
+    def rows_of(ref, at):
+        return ref.at[pl.ds(pl.multiple_of(at * 16, 16), 16)]
+
+    me_w = y * d.nx + x
     own_nodes = m.feat_grad.at[:, pl.ds(pl.multiple_of(c * 256, 256), 256)]
-    pltpu.make_async_copy(rows_of(m.summed, c), m.spread.at[c], recv.at[7]).start()
+    pltpu.make_async_copy(rows_of(m.summed, me_w), m.spread.at[me_w], recv.at[7]).start()
     pltpu.make_async_copy(rows_of(m.grad_slab, c), own_nodes, recv.at[8]).start()
 
-    def scatter(i):
-        to = peer_col(i)
-        remote(rows_of(m.summed, to), m.spread.at[c], send.at[7], recv.at[7], r, to).start()
-
-    def features(i):
-        to = peer_col(i)
-        remote(rows_of(m.grad_slab, to), own_nodes, send.at[8], recv.at[8], r, to).start()
-
-    each(1, d.ncol, scatter)
-    each(1, d.ncol, features)
+    def scatter(row, col, to_y, to_x):
+        src = rows_of(m.summed, to_y * d.nx + to_x)
+        remote(src, m.spread.at[me_w], send.at[7], recv.at[7], row, col).start()
+
+    def features(row, col, _):
+        remote(rows_of(m.grad_slab, col), own_nodes, send.at[8], recv.at[8], row, col).start()
+
+    peers_b(0, scatter)
+    peers_a(0, features)
     drain(m.spread, recv.at[7])
     total = m.spread[0].astype(F32)
-    for j in range(1, d.ncol):
+    for j in range(1, d.ncol_b):
         total += m.spread[j].astype(F32)
     m.mine[...] = total
-    pltpu.make_async_copy(m.mine, m.rows_all.at[y], recv.at[9]).start()
-
-    def along_y(i):
-        to = lax.rem(y + i, d.ny)
-        remote(m.mine, m.rows_all.at[y], send.at[9], recv.at[9], to * NK + k, c).start()
-
-    each(1, d.ny, along_y)
+    pltpu.make_async_copy(m.mine, m.rows_all.at[z], recv.at[9]).start()
+
+    def along_z(i):
+        to = lax.rem(z + i, d.nz)
+        remote(m.mine, m.rows_all.at[z], send.at[9], recv.at[9], r, to * d.nx + x).start()
+
+    each(1, d.nz, along_z)
     drain(m.rows_all, recv.at[9])
     total = m.rows_all[0]
-    for j in range(1, d.ny):
+    for j in range(1, d.nz):
         total += m.rows_all[j]
     m.final[...] = (total * scale).astype(BF)
-    own_rows_w = m.whole.at[k, pl.ds(pl.multiple_of(c * 16, 16), 16)]
+    own_rows_w = m.whole.at[k, pl.ds(pl.multiple_of(me_w * 16, 16), 16)]
     pltpu.make_async_copy(m.final, own_rows_w, recv.at[10]).start()
 
-    def publish(i):
-        to = peer_col(i)
-        remote(m.final, own_rows_w, send.at[10], recv.at[10], r, to).start()
-
-    each(1, d.ncol, publish)
+    def publish(row, col, to_y, to_x):
+        remote(m.final, own_rows_w, send.at[10], recv.at[10], row, col).start()
+
+    peers_b(0, publish)
     drain(m.whole.at[k], recv.at[10])
     share = remote(m.whole.at[k], m.whole.at[k], send.at[11], recv.at[11], twin_row, c)
     share.start()
     share.wait()
-    m.weight_grad[:, :half] = m.whole[0].astype(F32)
-    m.weight_grad[:, half:] = m.whole[1].astype(F32)
+    m.weight_raw[...] = m.whole[...]
     drain(m.slab.at[pl.ds(0, d.width - 16)], send.at[0])
     rest = pl.ds(0, d.na - 1)
     drain(m.out_a.at[rest, pl.ds(0, far_a)], send.at[1])
@@ -597,11 +631,19 @@
     drain(m.back_a.at[rest, :, pl.ds(0, near_a * BLK)], send.at[13])
     drain(m.back_b.at[rest, pl.ds(near_b * 16, (d.nz - near_b) * 16)], send.at[5])
     drain(m.back_b.at[rest, pl.ds(0, near_b * 16)], send.at[14])
-    drain(m.spread.at[pl.ds(0, d.ncol - 1)], send.at[7])
+    drain(m.spread.at[pl.ds(0, d.ncol_b - 1)], send.at[7])
     drain(m.grad_slab.at[pl.ds(0, d.width - 16)], send.at[8])
-    drain(m.rows_all.at[pl.ds(0, d.ny - 1)], send.at[9])
+    drain(m.rows_all.at[pl.ds(0, d.nz - 1)], send.at[9])
     drain(m.whole.at[0, pl.ds(0, d.width - 16)], send.at[10])
     drain(m.grad_slab, recv.at[8])
+
+
+def finish_kernel(mixed_in, feat_in, weight_in, mixed, feat_grad, weight_grad):
+    half = weight_in.shape[2]
+    mixed[...] = mixed_in[...]
+    feat_grad[...] = feat_in[...]
+    weight_grad[:, :half] = weight_in[0].astype(F32)
+    weight_grad[:, half:] = weight_in[1].astype(F32)
 
 
 def body(d, node_total, feats, weight, tile_vals, tile_src, tile_slot, slot_block, cotangent):
@@ -615,21 +657,25 @@
     inv = jnp.max(jnp.where(pair[:, None] == pair_ids[None, :], tile_ids[:, None], -1), axis=0)
     inputs = dict(
         inv=(inv, smem),
-        slot_flat=(slot_block.reshape(-1), smem),
-        slot_table=(slot_block, vmem),
-        feats=(feats, vmem),
-        weight=(weight, vmem),
-        tiles=(tile_vals, vmem),
-        cotangent=(cotangent, vmem),
+        slots=(slot_block.T, smem),
+        slot_table_in=(slot_block.T, anywhere),
+        feats=(feats, anywhere),
+        weight_in=(weight, anywhere),
+        tiles_in=(tile_vals, anywhere),
+        cotangent_in=(cotangent, anywhere),
     )
     outputs = dict(
         mixed=(sds(cotangent.shape, BF), vmem),
         feat_grad=(sds(feats.shape, BF), anywhere),
-        weight_grad=(sds((d.width, d.width), F32), vmem),
+        weight_raw=(sds((2, d.width, d.width // 2), BF), vmem),
     )
     half, dense_rows, hops_a, hops_b = d.width // 2, d.blocks * 8, max(1, d.ny // 2), max(1, d.nz // 2)
     dma = pltpu.SemaphoreType.DMA
     scratch = dict(
+        tiles=(tile_vals.shape, BF),
+        weight=((d.width, d.width), BF),
+        slot_table=((d.slots, d.slot_devices), jnp.int32),
+        cotangent=(cotangent.shape, BF),
         slab=((d.width, 256), BF),
         weight_t=((d.width, d.width), BF),
         proj=((d.width, 256), BF),
@@ -661,20 +707,21 @@
         grad_y=((d.width, 256), BF),
         grad_slab=((d.width, 256), BF),
         parts=((2, d.width, half), F32),
-        twin=((d.width, half), F32),
+        to_twin=((d.width, half), BF),
+        twin=((d.width, half), BF),
         summed=((d.width, half), BF),
-        spread=((d.ncol, 16, half), BF),
+        spread=((d.ncol_b, 16, half), BF),
         mine=((16, half), F32),
-        rows_all=((d.ny, 16, half), F32),
+        rows_all=((d.nz, 16, half), F32),
         final=((16, half), BF),
         whole=((2, d.width, half), BF),
     )
     semaphores = dict(
-        send=15, recv=15, send_ra=1, send_rb=1, recv_ra=4 * hops_a, recv_rb=4 * hops_b
+        send=15, recv=15, load=4, send_ra=1, send_rb=1, recv_ra=4 * hops_a, recv_rb=4 * hops_b
     )
     semaphores.update(recv_ga=4 * hops_a, recv_gb=4 * hops_b)
     names = tuple(inputs) + tuple(outputs) + tuple(scratch) + tuple(semaphores)
-    return pl.pallas_call(
+    mixed, feat_grad, weight_raw = pl.pallas_call(
         functools.partial(whole_kernel, d, 1.0 / math.sqrt(node_total), names),
         out_shape=tuple(v[0] for v in outputs.values()),
         in_specs=[v[1] for v in inputs.values()],
@@ -686,6 +733,15 @@
         ),
         name="layer",
     )(*(v[0] for v in inputs.values()))
+    return pl.pallas_call(
+        finish_kernel,
+        out_shape=(
+            sds(cotangent.shape, BF), sds(feats.shape, BF), sds((d.width, d.width), F32)
+        ),
+        in_specs=[vmem] * 3,
+        out_specs=(vmem,) * 3,
+        name="finish",
+    )(mixed, feat_grad, weight_raw)
 
 
 def solution(mesh):

time: 197 us -> 190 us (0.964)
  local copies, waits for them, and re-layouts: 6.11 us -> 0.66 us
    unnamed x8 -> x4, local copies, waits for them, and re-layouts: 5.37 us -> 0.66 us
    pallas_call x1, Pallas kernels: 189 us -> 185 us  [body(): pl.pallas_call(functools.partial(whole_kernel, d, 1.0 / math.sqrt(node_to...]
    pallas_call x0 -> x1, Pallas kernels: none -> 2.36 us  [body(): pl.pallas_call(finish_kernel, out_shape=(sds(cotangent.shape, BF), sds(fe...]
where the time goes in v2:
time: 190 us; the launch traced here: 189 us
  Pallas kernels  188 us (99%)
    pallas_call x1, Pallas kernels, body(): pl.pallas_call(functools.partial(whole_kernel, d, 1.0 / math.sqrt(node_to...  185 us

profile of v2, /device:TPU:1, one launch (start us, length us, event | category | flops | bytes accessed | tf_op | source)
XLA Modules:
  0.0 189.5 jit_solution(17974334499932263491)
XLA Ops:
  0.6 0.0 copy-start.1
  0.6 0.0 copy-start
  0.7 0.6 copy-done.1
  1.3 0.0 copy-done
  1.3 0.6 select_reduce_fusion.refs_0_
  1.9 185.2 %layer.1 = (bf16[16,8192]{1,0:T(8,128)(2,1)}, bf16[16,8192]{1,0:T(8,128)(2,1)}, bf16[2,512,256]{2,1,0:T(8,128)(2,1)}) custom-call(s32[64]{0:T(128)} %select_reduce_fusion.refs_0_, s32[32,512]{1,0:T(8,128)} %bitcast.3, s32[32,512]{1,0:T(8,128)} %bitcast.4, bf16[16,8192]{1,0:T(8,128)(2,1)} %refs_3_.1, bf16[512,512]{1,0:T(8,128)(2,1)} %refs_4_.1, ...), custom_call_target="tpu_custom_call" | custom-call | tf_op jit(solution)/shard_map/layer/pallas_call | solution.py:724
  187.1 2.4 %finish.1 = (bf16[16,8192]{1,0:T(8,128)(2,1)}, bf16[16,8192]{1,0:T(8,128)(2,1)}, f32[512,512]{1,0:T(8,128)}) custom-call(bf16[16,8192]{1,0:T(8,128)(2,1)} %get-tuple-element.6.mixed_in, bf16[16,8192]{1,0:T(8,128)(2,1)} %get-tuple-element.7.feat_in, bf16[2,512,256]{2,1,0:T(8,128)(2,1)} %get-tuple-element.8.weight_in), custom_call_target="tpu_custom_call" | custom-call | tf_op jit(solution)/shard_map/finish/pallas_call | solution.py:736
  (1 shorter events, 0.0 us)
Async XLA Ops:
  0.6 0.7 copy-start.1
  0.6 0.7 copy-start

commit v3 on v2

--- a/solution.py
+++ b/solution.py
@@ -86,12 +86,9 @@
     return jnp.where(offset > n // 2, 2 * offset - n, jnp.maximum(n - 1 - 2 * offset, 0))
 
 
-def far_count(n):
-    return max(1, n - 3)
-
-
-def near_start(n):
-    return max(1, n - 3)
+def parts_of(n):
+    ends = (0, max(1, n - 3), n - 1, n)
+    return [(a, b) for a, b in zip(ends, ends[1:]) if a < b]
 
 
 class Ring:
@@ -117,14 +114,14 @@
         at = self.at(way, piece, step)
         remote(src, dst, self.send.at[0], recv.at[at], row, col).start()
 
-    def reduce_step(self, step, dense, got, stage, last):
+    def reduce_step(self, step, dense, got, stage, part):
         for piece in range(2):
             for way in range(2):
                 hops = ways(self.n, way, piece)
                 if step >= hops:
                     continue
                 to = pos_of((1 - 2 * way) * (hops - step), self.n)
-                if (to >= far_count(self.n)) != last:
+                if not part[0] <= to < part[1]:
                     continue
                 if step == 0:
                     src = dense.at[to, self.rows(piece)]
@@ -245,15 +242,17 @@
     value = jnp.concatenate([value[:, 0], value[:, 1]], axis=0)
     m.proj[...] = value.reshape(d.width, 256).astype(BF)
 
-    far_a, far_b = far_count(d.ny), far_count(d.nz)
+    parts = parts_of(d.ny)
+    last_part = len(parts) - 1
+    spans = [pl.ds(a, b - a) for a, b in parts]
+    lane_spans = [pl.ds(a * BLK, (b - a) * BLK) for a, b in parts]
     lanes_of = [
         pl.ds(pl.multiple_of(pos_of(lax.rem(j - z + d.nz, d.nz), d.nz) * BLK, BLK), BLK)
         for j in range(d.nz)
     ]
 
     def send_b(group, late):
-        lanes = pl.ds(far_b * BLK, (d.nz - far_b) * BLK) if late else pl.ds(0, far_b * BLK)
-        sem = 3 if late else 2
+        lanes, sem = lane_spans[late], 15 + late
 
         def send_to(to_x):
             src = m.out_b.at[group * d.nx + to_x, :, lanes]
@@ -286,11 +285,10 @@
                 m.out_b[group * d.nx + to_x, :, lanes_of[to_z]] = packed[
                     d.ncol + to_z * d.nx + to_x
                 ]
-        send_b(group, False)
+        send_b(group, 0)
 
     def send_a(late):
-        part = pl.ds(far_a, d.ny - far_a) if late else pl.ds(0, far_a)
-        sem = 12 if late else 1
+        part, sem = spans[late], 12 + late
         dst = m.got_a.at[part, pl.ds(pl.multiple_of(me_a * 16, 16), 16)]
 
         def visit(row, col, to_k):
@@ -299,28 +297,26 @@
 
         return visit
 
-    for late in range(2):
+    for late in range(len(parts)):
         for first_k in range(2):
-            gk = k if first_k == 0 else 1 - k
-            for pos in range(far_a, d.ny) if late else range(far_a):
-                group_step(gk, pos)
-            if not late:
-                peers_a(first_k, send_a(False))
-    each(0, d.nrow, lambda i: send_b(lax.rem(r + i, d.nrow), True))
-    for other in range(NK):
-        peers_a(other, send_a(True))
-    for late in range(2):
-        part = pl.ds(far_a, d.ny - far_a) if late else pl.ds(0, far_a)
+            for pos in range(*parts[late]):
+                group_step(k_of[first_k], pos)
+            if late == 0:
+                peers_a(first_k, send_a(0))
+    for late in range(len(parts)):
+        if late:
+            each(0, d.nrow, lambda i: send_b(lax.rem(r + i, d.nrow), late))
+            for other in range(NK):
+                peers_a(other, send_a(late))
         pltpu.make_async_copy(
-            m.out_a.at[me_a, part],
-            m.got_a.at[part, pl.ds(pl.multiple_of(me_a * 16, 16), 16)],
-            recv.at[12 if late else 1],
+            m.out_a.at[me_a, spans[late]],
+            m.got_a.at[spans[late], pl.ds(pl.multiple_of(me_a * 16, 16), 16)],
+            recv.at[12 + late],
         ).start()
-        lanes = pl.ds(far_b * BLK, (d.nz - far_b) * BLK) if late else pl.ds(0, far_b * BLK)
         pltpu.make_async_copy(
-            m.out_b.at[me_b, :, lanes],
-            m.got_b.at[pl.ds(pl.multiple_of(me_b * 16, 16), 16), lanes],
-            recv.at[3 if late else 2],
+            m.out_b.at[me_b, :, lane_spans[late]],
+            m.got_b.at[pl.ds(pl.multiple_of(me_b * 16, 16), 16), lane_spans[late]],
+            recv.at[15 + late],
         ).start()
 
     lane = lax.broadcasted_iota(jnp.int32, (d.slot_devices, d.na * 16), 1)
@@ -378,21 +374,15 @@
         for pos in range(first, stop):
             m.dense_b[pos] = total[:, (pos - first) * BLK : (pos - first + 1) * BLK]
 
-    def rings(last):
-        for step in range(max(d.ny, d.nz) // 2):
-            ring_b.reduce_step(step, m.dense_b, m.ring_got_b, m.stage_b, last)
-            ring_a.reduce_step(step, m.dense_a, m.ring_got_a, m.stage_a, last)
-
-    drain(m.got_b.at[:, pl.ds(0, far_b * BLK)], recv.at[2])
-    aggregate_b(0, far_b)
-    drain(m.got_a.at[pl.ds(0, far_a)], recv.at[1])
-    each(0, far_a, aggregate_a)
-    rings(False)
-    drain(m.got_b.at[:, pl.ds(far_b * BLK, (d.nz - far_b) * BLK)], recv.at[3])
-    aggregate_b(far_b, d.nz)
-    drain(m.got_a.at[pl.ds(far_a, d.ny - far_a)], recv.at[12])
-    each(far_a, d.ny, aggregate_a)
-    rings(True)
+    for late, part in enumerate(parts):
+        drain(m.got_b.at[:, lane_spans[late]], recv.at[15 + late])
+        aggregate_b(*part)
+        drain(m.got_a.at[spans[late]], recv.at[12 + late])
+        each(part[0], part[1], aggregate_a)
+        for step in range(d.ny // 2):
+            ring_b.reduce_step(step, m.dense_b, m.ring_got_b, m.stage_b, part)
+            ring_a.reduce_step(step, m.dense_a, m.ring_got_a, m.stage_a, part)
+
     loads[3].wait()
 
     def widen_a(src, pos, piece):
@@ -445,13 +435,8 @@
             ring_a.gather_step(step, piece, m.all_a, widen_a)
             ring_b.gather_step(step, piece, m.all_b, widen_b)
 
-    near_a, near_b = near_start(d.ny), near_start(d.nz)
-
-    def columns(far):
-        if far:
-            return pl.ds(pl.multiple_of(k * d.ny * BLK, BLK), near_a * BLK)
-        at = pl.multiple_of((k * d.ny + near_a) * BLK, BLK)
-        return pl.ds(at, (d.ny - near_a) * BLK)
+    def columns(first, stop):
+        return pl.ds(pl.multiple_of((k * d.ny + first) * BLK, BLK), (stop - first) * BLK)
 
     def column(to_y):
         pos = pos_of(lax.rem(y - to_y + d.ny, d.ny), d.ny)
@@ -462,7 +447,7 @@
     ]
 
     def give_a(far, row, col, to_k):
-        first, stop = (0, near_a) if far else (near_a, d.ny)
+        first, stop = parts[far]
         a, device = to_k * d.ncol + col, row * d.ncol + col
         for pos in range(first, stop):
             rows = [
@@ -471,10 +456,10 @@
             ]
             m.back_a[a, :, pos * BLK : (pos + 1) * BLK] = jnp.concatenate(rows, axis=0).astype(BF)
         src = m.back_a.at[a, :, pl.ds(first * BLK, (stop - first) * BLK)]
-        return src, m.grads_a.at[pl.ds(pl.multiple_of(c * 16, 16), 16), columns(far)]
+        return src, m.grads_a.at[pl.ds(pl.multiple_of(c * 16, 16), 16), columns(first, stop)]
 
     def give_b(far, row, col, to_y, to_x):
-        first, stop = (0, near_b) if far else (near_b, d.nz)
+        first, stop = parts[far]
         b, device = row * d.nx + to_x, row * d.ncol + col
         at = [m.slots[r * CAP + cap, device] for cap in range(CAP)]
         for pos in range(first, stop):
@@ -485,7 +470,7 @@
         return src, m.grads_b.at[to_rows, column(to_y)]
 
     def give(far, other, start, stop):
-        sem_a, sem_b = (13, 14) if far else (4, 5)
+        sem_a, sem_b = 18 + far, 21 + far
 
         def visit_a(row, col, to_k):
             src, dst = give_a(far, row, col, to_k)
@@ -504,47 +489,62 @@
         each(max(1, start), stop, both_lines)
 
     def keep(far):
-        sem_a, sem_b = (13, 14) if far else (4, 5)
+        sem_a, sem_b = 18 + far, 21 + far
         src, dst = give_a(far, r, c, k)
         pltpu.make_async_copy(src, dst, recv.at[sem_a]).start()
         src, dst = give_b(far, r, c, y, x)
         pltpu.make_async_copy(src, dst, recv.at[sem_b]).start()
 
-    top, mid = max(d.ny, d.nz) // 2, d.ny // 2
+    top, mid = d.ny // 2, d.ny // 2
+    own, far = last_part, 0
+    give(own, 0, 0, d.ny)
     gathers(1)
-    give(False, 0, 0, mid)
-    if top >= 2:
+    give(own, 1, 0, d.ny)
+    if len(parts) > 2:
+        give(1, 0, 0, mid)
         gathers(2)
-    give(False, 0, mid, d.ny)
-    if top >= 3:
+        give(1, 0, mid, d.ny)
         gathers(3)
-    give(False, 1, 0, mid)
-    if top >= 4:
+        give(1, 1, 0, mid)
         gathers(4)
-    give(False, 1, mid, d.ny)
-    give(True, 0, 0, d.ny)
-    give(True, 1, 0, d.ny)
-    keep(False)
-    keep(True)
+        give(1, 1, mid, d.ny)
+    give(far, 0, 0, d.ny)
+    give(far, 1, 0, d.ny)
+    for part in range(len(parts)):
+        keep(part)
 
     span = d.ny * BLK
-    drain(m.grads_a.at[:, pl.ds(0, NK * (d.ny - near_a) * BLK)], recv.at[4])
-    for half_k in range(NK):
-        lanes = slice(half_k * span + near_a * BLK, (half_k + 1) * span)
-        value = jnp.dot(m.grads_a[:, lanes], m.matrix[lanes, :], preferred_element_type=F32)
-        m.wide[0] = value if half_k == 0 else m.wide[0] + value
-    drain(m.grads_b.at[pl.ds(0, d.nx * (d.nz - near_b) * 16)], recv.at[5])
-    for to_x in range(d.nx):
-        rows = slice((to_x * d.nz + near_b) * 16, (to_x + 1) * d.nz * 16)
-        m.wide[1, rows] = jnp.dot(m.grads_b[rows], m.matrix[...], preferred_element_type=F32)
-    drain(m.grads_a.at[:, pl.ds(0, NK * near_a * BLK)], recv.at[13])
-    for half_k in range(NK):
-        lanes = slice(half_k * span, half_k * span + near_a * BLK)
-        m.wide[0] += jnp.dot(m.grads_a[:, lanes], m.matrix[lanes, :], preferred_element_type=F32)
-    drain(m.grads_b.at[pl.ds(0, d.nx * near_b * 16)], recv.at[14])
-    for to_x in range(d.nx):
-        rows = slice(to_x * d.nz * 16, (to_x * d.nz + near_b) * 16)
-        m.wide[1, rows] = jnp.dot(m.grads_b[rows], m.matrix[...], preferred_element_type=F32)
+    near = parts[0][1]
+
+    def multiply(first, stop, fresh):
+        for half_k in range(NK):
+            lanes = slice(half_k * span + first * BLK, half_k * span + stop * BLK)
+            value = jnp.dot(m.grads_a[:, lanes], m.matrix[lanes, :], preferred_element_type=F32)
+            m.wide[0] = value if fresh and half_k == 0 else m.wide[0] + value
+        rows = jnp.concatenate(
+            [
+                m.grads_b[(j * d.nz + first) * 16 : (j * d.nz + stop) * 16]
+                for j in range(d.nx)
+            ],
+            axis=0,
+        )
+        value = jnp.dot(rows, m.matrix[...], preferred_element_type=F32)
+        count = (stop - first) * 16
+        for j in range(d.nx):
+            m.wide[1, (j * d.nz + first) * 16 : (j * d.nz + stop) * 16] = value[
+                j * count : (j + 1) * count
+            ]
+
+    def arrived(part):
+        count = parts[part][1] - parts[part][0]
+        drain(m.grads_a.at[:, pl.ds(0, NK * count * BLK)], recv.at[18 + part])
+        drain(m.grads_b.at[pl.ds(0, d.nx * count * 16)], recv.at[21 + part])
+
+    for part in range(1, len(parts)):
+        arrived(part)
+    multiply(near, d.ny, True)
+    arrived(0)
+    multiply(0, near, False)
 
     def join(path):
         value = m.wide[path].reshape(d.ncol, CAP, 8, 4 * BLK)
@@ -620,17 +620,14 @@
     m.weight_raw[...] = m.whole[...]
     drain(m.slab.at[pl.ds(0, d.width - 16)], send.at[0])
     rest = pl.ds(0, d.na - 1)
-    drain(m.out_a.at[rest, pl.ds(0, far_a)], send.at[1])
-    drain(m.out_a.at[rest, pl.ds(far_a, d.ny - far_a)], send.at[12])
-    drain(m.out_b.at[rest, :, pl.ds(0, far_b * BLK)], send.at[2])
-    drain(m.out_b.at[rest, :, pl.ds(far_b * BLK, (d.nz - far_b) * BLK)], send.at[3])
+    for part, (first, stop) in enumerate(parts):
+        drain(m.out_a.at[rest, spans[part]], send.at[12 + part])
+        drain(m.out_b.at[rest, :, lane_spans[part]], send.at[15 + part])
+        drain(m.back_a.at[rest, :, lane_spans[part]], send.at[18 + part])
+        drain(m.back_b.at[rest, pl.ds(first * 16, (stop - first) * 16)], send.at[21 + part])
     for ring, got, sem in ((ring_a, m.ring_got_a, m.send_ra), (ring_b, m.ring_got_b, m.send_rb)):
         for _ in range(2):
             drain(got.at[pl.ds(0, ring.copies())], sem.at[0])
-    drain(m.back_a.at[rest, :, pl.ds(near_a * BLK, (d.ny - near_a) * BLK)], send.at[4])
-    drain(m.back_a.at[rest, :, pl.ds(0, near_a * BLK)], send.at[13])
-    drain(m.back_b.at[rest, pl.ds(near_b * 16, (d.nz - near_b) * 16)], send.at[5])
-    drain(m.back_b.at[rest, pl.ds(0, near_b * 16)], send.at[14])
     drain(m.spread.at[pl.ds(0, d.ncol_b - 1)], send.at[7])
     drain(m.grad_slab.at[pl.ds(0, d.width - 16)], send.at[8])
     drain(m.rows_all.at[pl.ds(0, d.nz - 1)], send.at[9])
@@ -717,7 +714,7 @@
         whole=((2, d.width, half), BF),
     )
     semaphores = dict(
-        send=15, recv=15, load=4, send_ra=1, send_rb=1, recv_ra=4 * hops_a, recv_rb=4 * hops_b
+        send=24, recv=24, load=4, send_ra=1, send_rb=1, recv_ra=4 * hops_a, recv_rb=4 * hops_b
     )
     semaphores.update(recv_ga=4 * hops_a, recv_gb=4 * hops_b)
     names = tuple(inputs) + tuple(outputs) + tuple(scratch) + tuple(semaphores)

time: 190 us -> 188 us (0.989)
  Pallas kernels: 188 us -> 186 us
where the time goes in v3:
time: 188 us
  Pallas kernels  186 us (99%)
    pallas_call x1, Pallas kernels, body(): pl.pallas_call(functools.partial(whole_kernel, d, 1.0 / math.sqrt(node_to...  184 us

profile of v3, /device:TPU:1, one launch (start us, length us, event | category | flops | bytes accessed | tf_op | source)
XLA Modules:
  0.0 188.1 jit_solution(13698677977789933344)
XLA Ops:
  0.6 0.0 copy-start.1
  0.6 0.0 copy-start
  0.7 0.6 copy-done.1
  1.3 0.0 copy-done
  1.3 0.6 select_reduce_fusion.refs_0_
  1.9 183.8 %layer.1 = (bf16[16,8192]{1,0:T(8,128)(2,1)}, bf16[16,8192]{1,0:T(8,128)(2,1)}, bf16[2,512,256]{2,1,0:T(8,128)(2,1)}) custom-call(s32[64]{0:T(128)} %select_reduce_fusion.refs_0_, s32[32,512]{1,0:T(8,128)} %bitcast.3, s32[32,512]{1,0:T(8,128)} %bitcast.4, bf16[16,8192]{1,0:T(8,128)(2,1)} %refs_3_.1, bf16[512,512]{1,0:T(8,128)(2,1)} %refs_4_.1, ...), custom_call_target="tpu_custom_call" | custom-call | tf_op jit(solution)/shard_map/layer/pallas_call | solution.py:721
  185.7 2.4 %finish.1 = (bf16[16,8192]{1,0:T(8,128)(2,1)}, bf16[16,8192]{1,0:T(8,128)(2,1)}, f32[512,512]{1,0:T(8,128)}) custom-call(bf16[16,8192]{1,0:T(8,128)(2,1)} %get-tuple-element.6.mixed_in, bf16[16,8192]{1,0:T(8,128)(2,1)} %get-tuple-element.7.feat_in, bf16[2,512,256]{2,1,0:T(8,128)(2,1)} %get-tuple-element.8.weight_in), custom_call_target="tpu_custom_call" | custom-call | tf_op jit(solution)/shard_map/finish/pallas_call | solution.py:733
  (1 shorter events, 0.0 us)
Async XLA Ops:
  0.6 0.7 copy-start.1
  0.6 0.7 copy-start

commit v4 on v3

--- a/solution.py
+++ b/solution.py
@@ -52,12 +52,12 @@
     pltpu.make_async_copy(ref, ref, sem).wait()
 
 
-def each(start, stop, step):
+def each(start, stop, step, unroll=1):
     def run(i, carry):
         step(i)
         return carry
 
-    lax.fori_loop(start, stop, run, 0)
+    lax.fori_loop(start, stop, run, 0, unroll=unroll)
 
 
 def greet(barrier, row, col):
@@ -303,11 +303,15 @@
                 group_step(k_of[first_k], pos)
             if late == 0:
                 peers_a(first_k, send_a(0))
+
+    def bulk(late, other):
+        first = other * d.nrow // NK
+        each(first, first + d.nrow // NK, lambda i: send_b(lax.rem(r + i, d.nrow), late))
+        peers_a(other, send_a(late))
+
+    pending = [(late, other) for late in range(1, len(parts)) for other in range(NK)]
+    bulk(*pending.pop(0))
     for late in range(len(parts)):
-        if late:
-            each(0, d.nrow, lambda i: send_b(lax.rem(r + i, d.nrow), late))
-            for other in range(NK):
-                peers_a(other, send_a(late))
         pltpu.make_async_copy(
             m.out_a.at[me_a, spans[late]],
             m.got_a.at[spans[late], pl.ds(pl.multiple_of(me_a * 16, 16), 16)],
@@ -382,6 +386,10 @@
         for step in range(d.ny // 2):
             ring_b.reduce_step(step, m.dense_b, m.ring_got_b, m.stage_b, part)
             ring_a.reduce_step(step, m.dense_a, m.ring_got_a, m.stage_a, part)
+            if pending:
+                bulk(*pending.pop(0))
+        while pending:
+            bulk(*pending.pop(0))
 
     loads[3].wait()
 
@@ -424,7 +432,7 @@
             m.all_a[y, rows] = jnp.concatenate(low, axis=0).astype(BF)
             m.all_b[z, rows] = jnp.concatenate(high, axis=0).astype(BF)
 
-        each(first, first + d.blocks // 4, activate)
+        each(first, first + d.blocks // 4, activate, 2)
         ring_a.gather_step(0, piece, m.all_a, widen_a)
         ring_b.gather_step(0, piece, m.all_b, widen_b)
         widen_a(y, d.ny - 1, piece)

time: 188 us -> 198 us (1.053)
  Pallas kernels: 186 us -> 195 us
    pallas_call x1, Pallas kernels: 184 us -> 193 us  [body(): pl.pallas_call(functools.partial(whole_kernel, d, 1.0 / math.sqrt(node_to...]
where the time goes in v4:
time: 198 us; the launch traced here: 197 us
  Pallas kernels  195 us (98%)
    pallas_call x1, Pallas kernels, body(): pl.pallas_call(functools.partial(whole_kernel, d, 1.0 / math.sqrt(node_to...  193 us

profile of v4, /device:TPU:1, one launch (start us, length us, event | category | flops | bytes accessed | tf_op | source)
XLA Modules:
  0.0 197.4 jit_solution(7664322553020802467)
XLA Ops:
  0.6 0.0 copy-start.1
  0.6 0.0 copy-start
  0.7 0.6 copy-done.1
  1.3 0.0 copy-done
  1.3 0.6 select_reduce_fusion.refs_0_
  1.9 193.1 %layer.1 = (bf16[16,8192]{1,0:T(8,128)(2,1)}, bf16[16,8192]{1,0:T(8,128)(2,1)}, bf16[2,512,256]{2,1,0:T(8,128)(2,1)}) custom-call(s32[64]{0:T(128)} %select_reduce_fusion.refs_0_, s32[32,512]{1,0:T(8,128)} %bitcast.3, s32[32,512]{1,0:T(8,128)} %bitcast.4, bf16[16,8192]{1,0:T(8,128)(2,1)} %refs_3_.1, bf16[512,512]{1,0:T(8,128)(2,1)} %refs_4_.1, ...), custom_call_target="tpu_custom_call" | custom-call | tf_op jit(solution)/shard_map/layer/pallas_call | solution.py:729
  195.0 2.4 %finish.1 = (bf16[16,8192]{1,0:T(8,128)(2,1)}, bf16[16,8192]{1,0:T(8,128)(2,1)}, f32[512,512]{1,0:T(8,128)}) custom-call(bf16[16,8192]{1,0:T(8,128)(2,1)} %get-tuple-element.6.mixed_in, bf16[16,8192]{1,0:T(8,128)(2,1)} %get-tuple-element.7.feat_in, bf16[2,512,256]{2,1,0:T(8,128)(2,1)} %get-tuple-element.8.weight_in), custom_call_target="tpu_custom_call" | custom-call | tf_op jit(solution)/shard_map/finish/pallas_call | solution.py:741
  (1 shorter events, 0.0 us)
Async XLA Ops:
  0.6 0.7 copy-start.1
  0.6 0.7 copy-start
